TPU v7x, 32 devices: a whole 2x2x4 slice. The times are simulated.
32 devices in a mesh: fsdp: 16 (over z, y, x), tp: 2 (over core).
Axes of the slice: x: 2, y: 2, z: 4, core: 2. Of those that a mesh axis runs over, the one named last changes fastest.
Arguments:
- tokens: bfloat16 [12608, 768], P(('fsdp', 'tp')), may hold values from -6 to 6
- cotangent: bfloat16 [12608, 768], P(('fsdp', 'tp')), may hold values from -6 to 6
- image_counts: int32 [16], P('fsdp'), may hold values from 1 to 4, as said below
- w_qkv: bfloat16 [3, 768, 768], P(None, 'fsdp', 'tp'), may hold values from -0.21875 to 0.21875
- b_query: float32 [768], P('tp'), may hold values from -3 to 3
- b_value: float32 [768], P('tp'), may hold values from -3 to 3
- w_out: bfloat16 [768, 768], P('tp', 'fsdp'), may hold values from -0.75 to 0.75
- b_out: float32 [768], replicated, may hold values from -3 to 3
- w_up: bfloat16 [768, 3072], P('fsdp', 'tp'), may hold values from -0.21875 to 0.21875
- b_up: float32 [3072], P('tp'), may hold values from -3 to 3
- w_down: bfloat16 [3072, 768], P('tp', 'fsdp'), may hold values from -0.15625 to 0.15625
- b_down: float32 [768], replicated, may hold values from -3 to 3
- gain_one: float32 [768], replicated, may hold values from 0.1 to 1.9
- shift_one: float32 [768], replicated, may hold values from -3 to 3
- gain_two: float32 [768], replicated, may hold values from 0.1 to 1.9
- shift_two: float32 [768], replicated, may hold values from -3 to 3
Outputs:
- block_out: bfloat16 [12608, 768], P(('fsdp', 'tp'))
- grad_tokens: float32 [12608, 768], P(('fsdp', 'tp'))
- grad_qkv: float32 [3, 768, 768], P(None, 'fsdp', 'tp')
- grad_out: float32 [768, 768], P('tp', 'fsdp')
- grad_up: float32 [768, 3072], P('fsdp', 'tp')
- grad_down: float32 [3072, 768], P('tp', 'fsdp')
- grad_b_query: float32 [768], P('tp')
- grad_b_value: float32 [768], P('tp')
- grad_b_out: float32 [768], replicated
- grad_b_up: float32 [3072], P('tp')
- grad_b_down: float32 [768], replicated
- grad_gain_one: float32 [768], replicated
- grad_shift_one: float32 [768], replicated
- grad_gain_two: float32 [768], replicated
- grad_shift_two: float32 [768], replicated
Inputs may be any that keep to these rules, and one draw needn't show every extreme that they name: `image_counts`: entry f counts the live images among the 4 slots of index f of fsdp; live images come first; entry 0 equals 4.
All inputs are finite; a program needn't handle non-finite values.
Results may differ from a plain program's by a relative error of at most 0.015.
Values may be sent and summed in bfloat16 or wider, within the bound.
A program may use at most 128 MiB of HBM per device.

v0:
```python
import functools

import jax
import jax.numpy as jnp
from jax import lax
from jax.experimental import pallas as pl
from jax.experimental.pallas import tpu as pltpu
from jax.sharding import PartitionSpec as P

HEAD_DIM = 64
SEQ = 197


EPS = 1e-06
INV_ROOT_TWO = 0.7071067811865476
INV_ROOT_TWO_PI = 0.3989422804014327
BF = jnp.bfloat16
F32 = jnp.float32


def layer_norm(values, gain, shift):
    center = values - jnp.mean(values, axis=-1, keepdims=True)
    scale_inv = lax.rsqrt(jnp.mean(center * center, axis=-1, keepdims=True) + EPS)
    normal = center * scale_inv
    return (normal, scale_inv, normal * gain + shift)


def norm_back(incoming, normal, scale_inv, gain):
    scaled = incoming * gain
    return scale_inv * (
        scaled
        - jnp.mean(scaled, axis=-1, keepdims=True)
        - normal * jnp.mean(scaled * normal, axis=-1, keepdims=True)
    )


def gelu_parts(pre):
    cdf = 0.5 * (1.0 + lax.erf(pre * INV_ROOT_TWO))
    dens = jnp.exp(-0.5 * pre * pre) * INV_ROOT_TWO_PI
    return (pre * cdf, cdf + pre * dens)


def dot_nn(left, right):
    return lax.dot_general(left, right, (((1,), (0,)), ((), ())), preferred_element_type=F32)


def dot_nt(left, right):
    return lax.dot_general(left, right, (((1,), (1,)), ((), ())), preferred_element_type=F32)


def dot_tn(left, right):
    return lax.dot_general(left, right, (((0,), (0,)), ((), ())), preferred_element_type=F32)


def score_of(query, key):
    return jnp.einsum("bqhe,bkhe->bhqk", query, key, preferred_element_type=F32) * HEAD_DIM ** (-0.5)


def attend(query, key, value):
    scores = score_of(query, key)
    peak = jnp.max(scores, axis=-1, keepdims=True)
    lse = peak + jnp.log(jnp.sum(jnp.exp(scores - peak), axis=-1, keepdims=True))
    probs = jnp.exp(scores - lse).astype(BF)
    attended = jnp.einsum("bhqk,bkhe->bqhe", probs, value, preferred_element_type=F32)
    return (attended.astype(BF), lse)


def attend_back(query, key, value, lse, attended, dattended):
    scale = HEAD_DIM ** (-0.5)
    delta = jnp.sum(dattended.astype(F32) * attended.astype(F32), axis=-1)
    delta = jnp.transpose(delta, (0, 2, 1))[..., None]
    probs_f = jnp.exp(score_of(query, key) - lse)
    probs = probs_f.astype(BF)
    dvalue = jnp.einsum("bhqk,bqhe->bkhe", probs, dattended, preferred_element_type=F32)
    dprobs = jnp.einsum("bqhe,bkhe->bhqk", dattended, value, preferred_element_type=F32)
    dscores = (probs_f * (dprobs - delta)).astype(BF)
    dquery = jnp.einsum("bhqk,bkhe->bqhe", dscores, key, preferred_element_type=F32) * scale
    dkey = jnp.einsum("bhqk,bqhe->bkhe", dscores, query, preferred_element_type=F32) * scale
    return (dquery, dkey, dvalue)


def swap(value, axis, bit):
    size = lax.axis_size(axis)
    return lax.ppermute(value, axis, [(i, i ^ (1 << bit)) for i in range(size)])


def bits_of(axis):
    return lax.axis_size(axis).bit_length() - 1


def by_bits(shard_rows):
    size = lax.axis_size("fsdp")
    return size & (size - 1) == 0 and shard_rows % 16 == 0


def order_of(first):
    count = bits_of("fsdp")
    rest = [b for b in range(count) if b not in first]
    return [b for b in first if b < count] + rest


def enter(count):
    me = lax.axis_index("fsdp")
    bits = [(me // (1 << b)) % 2 for b in range(count)]
    near = [{"fsdp": me + (1 - 2 * bits[b]) * (1 << b)} for b in range(count)]
    twin = {"tp": 1 - lax.axis_index("tp")}
    barrier = pltpu.get_barrier_semaphore()
    for device in near + [twin]:
        pl.semaphore_signal(barrier, inc=1, device_id=device, device_id_type=pl.DeviceIdType.MESH)
    pl.semaphore_wait(barrier, count + 1)
    return bits, near, twin


def place(bits, rel):
    return sum((1 - m if (rel >> b) & 1 else m) * (1 << b) for b, m in enumerate(bits))


def remote(src, dst, sems, at, device):
    return pltpu.make_async_remote_copy(
        src_ref=src,
        dst_ref=dst,
        send_sem=sems[0].at[at],
        recv_sem=sems[1].at[at],
        device_id=device,
        device_id_type=pl.DeviceIdType.MESH,
    )


def gather_kernel(count, steps, *refs):
    k = len(steps)
    shards, own, oth = refs[:k], refs[k : 2 * k], refs[2 * k : 3 * k]
    ring, pair, here = refs[3 * k : 3 * k + 2], refs[3 * k + 2 : 3 * k + 4], refs[3 * k + 4]
    size = 1 << count
    bits, near, twin = enter(count)
    copies = []

    def spread(c, rel, done):
        block = own[c].at[place(bits, rel)]
        src = shards[c] if rel == 0 else block
        for bit in steps[c][done:]:
            copies.append(remote(src, block, ring, c * size + (rel | 1 << bit), near[bit]))
            copies[-1].start()
        copies.append(remote(src, oth[c].at[place(bits, rel)], pair, c * size + rel, twin))
        copies[-1].start()

    keep = [pltpu.make_async_copy(shards[c], own[c].at[place(bits, 0)], here.at[c]) for c in range(k)]
    for c in range(k):
        spread(c, 0, 0)
        keep[c].start()
    held = [[0] for _ in range(k)]
    for step in range(count):
        for c in range(k):
            bit = steps[c][step]
            fresh = [rel | 1 << bit for rel in held[c]]
            for rel in fresh:
                block = own[c].at[place(bits, rel)]
                remote(block, block, ring, c * size + rel, near[bit]).wait_recv()
                spread(c, rel, step + 1)
            held[c] = held[c] + fresh
    for c in range(k):
        for rel in range(size):
            block = oth[c].at[place(bits, rel)]
            remote(block, block, pair, c * size + rel, twin).wait_recv()
        keep[c].wait()
    for copy in copies:
        copy.wait_send()


def gather_all(shards, firsts):
    if not by_bits(shards[0].shape[0]):
        own = [lax.all_gather(s, "fsdp", axis=0, tiled=True) for s in shards]
        return own, [swap(o, "tp", 0) for o in own]
    size, count, k = lax.axis_size("fsdp"), bits_of("fsdp"), len(shards)
    whole = [jax.ShapeDtypeStruct((size,) + s.shape, s.dtype) for s in shards]
    outs = pl.pallas_call(
        functools.partial(gather_kernel, count, [order_of(f)[::-1] for f in firsts]),
        out_shape=whole + whole,
        in_specs=[pl.BlockSpec(memory_space=pl.ANY)] * k,
        out_specs=[pl.BlockSpec(memory_space=pl.ANY)] * (2 * k),
        scratch_shapes=[pltpu.SemaphoreType.DMA((k * size,))] * 4 + [pltpu.SemaphoreType.DMA((k,))],
        compiler_params=pltpu.CompilerParams(collective_id=0, has_side_effects=True),
        name="gather_all",
    )(*shards)
    outs = [o.reshape((-1, o.shape[2])) for o in outs]
    return outs[:k], outs[k:]


def scatter_kernel(count, orders, *refs):
    k = len(orders)
    own, oth, out = refs[:k], refs[k : 2 * k], refs[2 * k : 3 * k]
    from_twin, sent, came = refs[3 * k : 4 * k], refs[4 * k : 5 * k], refs[5 * k : 6 * k]
    ring, pair = refs[6 * k : 6 * k + 2], refs[6 * k + 2 : 6 * k + 4]
    size = 1 << count
    bits, near, twin = enter(count)
    copies = []

    def stage(c, step):
        done = sum(1 << b for b in orders[c][:step])
        if step == count:
            return [0]
        return [r for r in range(size) if r & done == 0 and (r >> orders[c][step]) & 1]

    for step in range(count + 1):
        for c in range(k):
            for rel in stage(c, step):
                copy = remote(oth[c].at[place(bits, rel)], from_twin[c].at[rel], pair, c * size + rel, twin)
                copy.start()
                copies.append(copy)
    for step in range(count + 1):
        for c in range(k):
            for rel in stage(c, step):
                slot = from_twin[c].at[rel]
                remote(slot, slot, pair, c * size + rel, twin).wait_recv()
                total = own[c][place(bits, rel)].astype(F32) + from_twin[c][rel].astype(F32)
                for bit in orders[c][:step]:
                    at = rel | 1 << bit
                    slot = came[c].at[at]
                    remote(slot, slot, ring, c * size + at, near[bit]).wait_recv()
                    total = total + came[c][at].astype(F32)
                if step == count:
                    out[c][...] = total
                else:
                    sent[c][rel] = total.astype(BF)
                    copy = remote(
                        sent[c].at[rel], came[c].at[rel], ring, c * size + rel, near[orders[c][step]]
                    )
                    copy.start()
                    copies.append(copy)
    for copy in copies:
        copy.wait_send()


def scatter_all(owns, others, firsts):
    size = lax.axis_size("fsdp")
    rows = owns[0].shape[0] // size
    owns, others = [o.astype(BF) for o in owns], [o.astype(BF) for o in others]
    if not by_bits(rows):
        return [
            lax.psum_scatter(
                o.astype(F32) + swap(t, "tp", 0).astype(F32), "fsdp", scatter_dimension=0, tiled=True
            )
            for o, t in zip(owns, others)
        ]
    count, k = bits_of("fsdp"), len(owns)
    blocks = [(size, rows, o.shape[1]) for o in owns]
    return pl.pallas_call(
        functools.partial(scatter_kernel, count, [order_of(f) for f in firsts]),
        out_shape=[jax.ShapeDtypeStruct(b[1:], F32) for b in blocks],
        in_specs=[pl.BlockSpec(memory_space=pltpu.VMEM)] * k + [pl.BlockSpec(memory_space=pl.ANY)] * k,
        out_specs=[pl.BlockSpec(memory_space=pltpu.VMEM)] * k,
        scratch_shapes=[pltpu.VMEM(b, BF) for b in blocks] * 3
        + [pltpu.SemaphoreType.DMA((k * size,))] * 4,
        compiler_params=pltpu.CompilerParams(
            collective_id=1, has_side_effects=True, vmem_limit_bytes=48 * 1024 * 1024
        ),
        name="scatter_all",
    )(*[o.reshape(b) for o, b in zip(owns, blocks)], *[o.reshape(b) for o, b in zip(others, blocks)])


def all_sum(split_own, split_other, whole):
    mine = jnp.concatenate(split_own + whole)
    total = mine + swap(jnp.concatenate(split_other + whole), "tp", 0)
    size = lax.axis_size("fsdp")
    if size & (size - 1) == 0:
        for bit in range(bits_of("fsdp")):
            total = total + swap(total, "fsdp", bit)
    else:
        total = lax.psum(total, "fsdp")
    parts, at = [], 0
    for piece in split_own + whole:
        parts.append(total[at : at + piece.shape[0]])
        at += piece.shape[0]
    return parts


def local(
    tokens,
    cotangent,
    image_counts,
    w_qkv,
    b_query,
    b_value,
    w_out,
    b_out,
    w_up,
    b_up,
    w_down,
    b_down,
    gain_one,
    shift_one,
    gain_two,
    shift_two,
):
    rows, width = tokens.shape
    images = rows // SEQ
    slot = lax.axis_index("tp")
    line = (slot * rows + jnp.arange(rows, dtype=jnp.int32)) // SEQ
    live = (line < image_counts[0]).astype(F32)[:, None]
    head_width = w_qkv.shape[2]
    hidden = w_up.shape[1]
    heads = head_width // HEAD_DIM

    shard_qkv = jnp.concatenate([w_qkv[0], w_qkv[1], w_qkv[2]], axis=1)
    (qkv_own, mix_own, wd_own), (qkv_oth, mix_oth, wd_oth) = gather_all(
        [shard_qkv, jnp.concatenate([w_out.T, w_up], axis=1), w_down.T], [(0, 1), (1, 0), (2, 0)]
    )
    wo_own, wu_own = mix_own[:, :head_width], mix_own[:, head_width:]
    wo_oth, wu_oth = mix_oth[:, :head_width], mix_oth[:, head_width:]

    bias_own = jnp.concatenate([b_query, jnp.zeros_like(b_query), b_value, b_up])
    bias_oth = swap(bias_own, "tp", 0)
    cut = 3 * head_width

    xf = tokens.astype(F32)
    xh1, rs1, n1 = layer_norm(xf, gain_one, shift_one)
    h1 = n1.astype(BF)
    shape5 = (images, SEQ, 3, heads, HEAD_DIM)
    p_own = (dot_nn(h1, qkv_own) + bias_own[:cut]).astype(BF).reshape(shape5)
    p_oth = (dot_nn(h1, qkv_oth) + bias_oth[:cut]).astype(BF).reshape(shape5)
    q4, k4, v4 = [jnp.concatenate([p_own[:, :, j], p_oth[:, :, j]], axis=2) for j in range(3)]
    att4, lse = attend(q4, k4, v4)
    att_own = att4[:, :, :heads].reshape(rows, head_width)
    att_oth = att4[:, :, heads:].reshape(rows, head_width)
    mid = xf + (dot_nt(att_own, wo_own) + dot_nt(att_oth, wo_oth)) + b_out
    xh2, rs2, n2 = layer_norm(mid, gain_two, shift_two)
    h2 = n2.astype(BF)
    gel_own, slope_own = gelu_parts(dot_nn(h2, wu_own) + bias_own[cut:])
    gel_oth, slope_oth = gelu_parts(dot_nn(h2, wu_oth) + bias_oth[cut:])
    act_own, act_oth = gel_own.astype(BF), gel_oth.astype(BF)
    block_out = ((mid + (dot_nt(act_own, wd_own) + dot_nt(act_oth, wd_oth)) + b_down) * live).astype(BF)

    dout = (cotangent.astype(F32) * live).astype(BF)
    doutf = dout.astype(F32)
    dpre_own = dot_nn(dout, wd_own) * slope_own
    dpre_oth = dot_nn(dout, wd_oth) * slope_oth
    dpo, dpt = dpre_own.astype(BF), dpre_oth.astype(BF)
    dn2 = dot_nt(dpo, wu_own) + dot_nt(dpt, wu_oth)
    dmid = doutf + norm_back(dn2, xh2, rs2, gain_two)
    dmid_b = dmid.astype(BF)
    part_bup, sum_bdown, sum_gain2, sum_shift2, sum_bout = all_sum(
        [jnp.sum(dpre_own, axis=0)],
        [jnp.sum(dpre_oth, axis=0)],
        [jnp.sum(doutf, axis=0), jnp.sum(dn2 * xh2, axis=0), jnp.sum(dn2, axis=0), jnp.sum(dmid, axis=0)],
    )
    shape4 = (images, SEQ, heads, HEAD_DIM)
    datt = jnp.concatenate(
        [
            dot_nn(dmid_b, wo_own).astype(BF).reshape(shape4),
            dot_nn(dmid_b, wo_oth).astype(BF).reshape(shape4),
        ],
        axis=2,
    )
    dq4, dk4, dv4 = attend_back(q4, k4, v4, lse, att4, datt)
    g_bq = jnp.sum(dq4, axis=(0, 1)).reshape(2 * head_width)
    g_bv = jnp.sum(dv4, axis=(0, 1)).reshape(2 * head_width)
    d5 = jnp.stack([dq4.astype(BF), dk4.astype(BF), dv4.astype(BF)], axis=2)
    d_own = d5[:, :, :, :heads].reshape(rows, cut)
    d_oth = d5[:, :, :, heads:].reshape(rows, cut)
    dn1 = dot_nt(d_own, qkv_own) + dot_nt(d_oth, qkv_oth)
    grad_tokens = dmid + norm_back(dn1, xh1, rs1, gain_one)
    part_bq, part_bv, sum_gain1, sum_shift1 = all_sum(
        [g_bq[:head_width], g_bv[:head_width]],
        [g_bq[head_width:], g_bv[head_width:]],
        [jnp.sum(dn1 * xh1, axis=0), jnp.sum(dn1, axis=0)],
    )
    s_heads, s_up, s_down = scatter_all(
        [
            jnp.concatenate([dot_tn(h1, d_own).astype(BF), dot_tn(dmid_b, att_own).astype(BF)], axis=1),
            dot_tn(h2, dpo),
            dot_tn(dout, act_own),
        ],
        [
            jnp.concatenate([dot_tn(h1, d_oth).astype(BF), dot_tn(dmid_b, att_oth).astype(BF)], axis=1),
            dot_tn(h2, dpt),
            dot_tn(dout, act_oth),
        ],
        [(0, 1), (1, 0), (2, 0)],
    )
    s_qkv, s_out = s_heads[:, :cut], s_heads[:, cut:]
    return (
        block_out,
        grad_tokens,
        jnp.stack([s_qkv[:, j * head_width : (j + 1) * head_width] for j in range(3)]),
        s_out.T,
        s_up,
        s_down.T,
        part_bq,
        part_bv,
        sum_bout,
        part_bup,
        sum_bdown,
        sum_gain1,
        sum_shift1,
        sum_gain2,
        sum_shift2,
    )


def solution(mesh):
    return jax.shard_map(
        local,
        mesh=mesh,
        in_specs=(
            P(("fsdp", "tp"), None),
            P(("fsdp", "tp"), None),
            P("fsdp"),
            P(None, "fsdp", "tp"),
            P("tp"),
            P("tp"),
            P("tp", "fsdp"),
            P(),
            P("fsdp", "tp"),
            P("tp"),
            P("tp", "fsdp"),
            P(),
            P(),
            P(),
            P(),
            P(),
        ),
        out_specs=(
            P(("fsdp", "tp"), None),
            P(("fsdp", "tp"), None),
            P(None, "fsdp", "tp"),
            P("tp", "fsdp"),
            P("fsdp", "tp"),
            P("tp", "fsdp"),
            P("tp"),
            P("tp"),
            P(),
            P("tp"),
            P(),
            P(),
            P(),
            P(),
            P(),
        ),
        check_vma=False,
    )
```

profile of v0, /device:TPU:0, one launch (start us, length us, event | category | flops | bytes accessed | tf_op | source)
XLA Modules:
  0.0 322.2 jit_solution(7645080231144743214)
XLA Ops:
  3.5 1.2 convert_reduce_fusion
  4.7 1.4 fusion.41
  6.2 1.5 pad_maximum_fusion.16.refs_1_
  8.3 66.5 %gather_all.1 = (bf16[16,48,1152]{2,1,0:T(8,128)(2,1)}, bf16[16,48,1920]{2,1,0:T(8,128)(2,1)}, bf16[16,48,1536]{2,1,0:T(8,128)(2,1)}, bf16[16,48,1152]{2,1,0:T(8...) custom-call(bf16[48,1152]{1,0:T(8,128)(2,1)} %pad_maximum_fusion.17.refs_0_, ...), custom_call_target="tpu_custom_call" | custom-call | tf_op jit(solution)/shard_map/gather_all/pallas_call | solution.py:175
  74.8 3.5 %fusion.1 = bf16[394,1152]{1,0:T(8,128)(2,1)} fusion(bf16[768,1152]{1,0:T(8,128)(2,1)} %bitcast.138, f32[1152]{0:T(1024)S(1)} %pad_maximum_fusion.23, bf16[394,768]{1,0:T(8,128)(2,1)S(1)} %copy-done.5, f32[768]{0:T(1024)S(1)} %copy-done.43, f32[768]{0:T(1024)S(1)} %copy-done.36, f32[394]{0:T(512)S(1)} %add_rsqrt_fusion.1, f32[394]{0:T(512)S(1)} %broadcast_multiply_fusion.5), kind=kOutput, calls=%fused_computation.16 | convolution fusion | flops 699895296 | bytes 3296336 | tf_op jit(solution)/shard_map/dot_general | solution.py:44
  78.3 3.3 %reshape.192 = bf16[2,197,3,6,64]{4,3,2,1,0:T(8,128)(2,1)S(1)} reshape(bf16[394,1152]{1,0:T(8,128)(2,1)} %fusion.1) | data formatting | bytes 1815552 | tf_op jit(solution)/shard_map/reshape | solution.py:318
  81.7 1.6 fusion.78
  84.1 2.3 copy.86
  86.3 2.2 copy.84
  89.0 3.5 %add_convert_fusion = bf16[394,1152]{1,0:T(8,128)(2,1)} fusion(f32[1152]{0:T(1024)S(1)} %slice.167, bf16[768,1152]{1,0:T(8,128)(2,1)} %bitcast.136, bf16[394,768]{1,0:T(8,128)(2,1)S(1)} %copy-done.5, f32[768]{0:T(1024)S(1)} %copy-done.43, f32[768]{0:T(1024)S(1)} %copy-done.36, f32[394]{0:T(512)S(1)} %add_rsqrt_fusion.1, f32[394]{0:T(512)S(1)} %broadcast_multiply_fusion.5), kind=kOutput, calls=%fused_computation.40 | convolution fusion | flops 699895296 | bytes 3296336 | tf_op jit(solution)/shard_map/dot_general | solution.py:44
  92.6 3.0 reshape.193
  95.6 1.6 fusion.79
  97.2 1.6 copy.85
  98.8 1.2 copy.87
  100.0 2.1 multiply_reduce_fusion
  103.0 1.3 copy-done
  104.8 3.5 %fusion.32 = bf16[2,197,12,64]{1,3,2,0:T(8,128)(2,1)S(1)} fusion(bf16[2,197,6,64]{1,3,2,0:T(8,128)(2,1)S(1)} %bitcast.108, bf16[2,197,6,64]{1,3,2,0:T(8,128)(2,1)S(1)} %bitcast.106, f32[2,12,197,197]{2,3,1,0:T(8,128)} %copy-done, f32[2,12,197]{2,1,0:T(8,128)S(1)} %log_add_fusion), kind=kOutput, calls=%fused_computation.71 | convolution fusion | flops 122620680 | bytes 4954944 | tf_op jit(solution)/shard_map/bhqk,bkhe->bqhe/dot_general | solution.py:64
  109.5 1.0 reshape.174
  110.5 1.4 copy.54
  112.2 1.9 fusion.51
  114.1 1.8 fusion.87
  116.5 1.7 copy-done.32
  118.1 2.4 multiply_convert_fusion.2
  120.5 14.8 %multiply_convert_fusion.1 = (bf16[394,1536]{1,0:T(8,128)(2,1)}, f32[394,1536]{1,0:T(8,128)S(1)}) fusion(f32[1536]{0:T(1024)S(1)} %slice.179, bf16[394,768]{1,0:T(8,128)(2,1)S(1)} %add_convert_fusion.1, bf16[768,1920]{1,0:T(8,128)(2,1)S(1)} %bitcast.124), kind=kOutput, calls=%fused_computation.26 | convolution fusion | flops 933193728 | bytes 6612992 | tf_op jit(solution)/shard_map/dot_general | solution.py:44
  135.3 1.8 fusion.89
  137.1 1.1 fusion.15
  139.2 1.9 fusion.88
  141.1 1.6 multiply_reduce_fusion.2
  143.4 1.3 convolution_convert_fusion.10
  144.7 1.2 convolution_convert_fusion.9
  145.9 2.3 reshape.190
  148.3 1.5 copy.57
  149.8 2.3 reshape.191
  152.1 1.5 copy.58
  154.0 4.2 %multiply_convert_fusion = bf16[2,12,197,197]{2,3,1,0:T(8,128)(2,1)S(1)} fusion(f32[2,12,197,197]{2,3,1,0:T(8,128)} %copy-done, f32[2,12,197]{2,1,0:T(8,128)S(1)} %bitcast.122, f32[2,12,197]{2,1,0:T(8,128)S(1)} %log_add_fusion, bf16[2,197,6,64]{1,3,2,0:T(8,128)(2,1)S(1)} %bitcast.109, bf16[2,197,6,64]{1,3,2,0:T(8,128)(2,1)S(1)} %bitcast.107, ...), kind=kOutput, calls=%fused_computation | convolution fusion | flops 124483512 | bytes 6836688 | tf_op jit(solution)/shard_map/bqhe,bkhe->bhqk/dot_general | solution.py:75
  160.1 1.2 bitcast_reduce_fusion
  161.6 2.8 convolution_convert_fusion.3
  164.4 1.5 convolution_convert_fusion.7
  165.9 1.4 convolution_convert_fusion.5
  168.1 1.2 fusion.80
  169.3 2.2 copy.63
  171.5 4.3 %reshape.182 = bf16[394,1152]{0,1:T(8,128)(2,1)} reshape(bf16[2,197,3,6,64]{1,0,4,3,2:T(2,128)(2,1)} %copy.63) | data formatting | bytes 1815552 | tf_op jit(solution)/shard_map/reshape | solution.py:357
  175.9 4.2 %fusion.91 = f32[394,768]{1,0:T(8,128)} fusion(bf16[394,1152]{0,1:T(8,128)(2,1)} %reshape.182, bf16[768,1152]{1,0:T(8,128)(2,1)} %bitcast.139), kind=kOutput, calls=%fused_computation.175 | convolution fusion | flops 697171968 | bytes 3887616 | tf_op jit(solution)/shard_map/dot_general | solution.py:48
  180.0 2.7 convolution_convert_fusion.1
  182.8 2.9 convolution_convert_fusion.4
  185.7 2.2 fusion.90
  188.6 2.2 copy.64
  190.8 4.1 %reshape.183 = bf16[394,1152]{0,1:T(8,128)(2,1)} reshape(bf16[2,197,3,6,64]{1,0,4,3,2:T(2,128)(2,1)} %copy.64) | data formatting | bytes 1815552 | tf_op jit(solution)/shard_map/reshape | solution.py:358
  194.9 4.1 %convolution_convert_fusion = bf16[768,1152]{1,0:T(8,128)(2,1)} fusion(bf16[394,1152]{0,1:T(8,128)(2,1)} %reshape.183, bf16[394,768]{1,0:T(8,128)(2,1)S(1)} %copy-done.5, f32[768]{0:T(1024)S(1)} %copy-done.43, f32[768]{0:T(1024)S(1)} %copy-done.36, f32[394]{0:T(512)S(1)} %add_rsqrt_fusion.1, f32[394]{0:T(512)S(1)} %broadcast_multiply_fusion.5), kind=kOutput, calls=%fused_computation.7 | convolution fusion | flops 699872256 | bytes 3291728 | tf_op jit(solution)/shard_map/dot_general | solution.py:52
  199.0 2.6 fusion.40
  201.9 4.6 %convolution_convert_fusion.2 = bf16[768,1536]{1,0:T(8,128)(2,1)} fusion(bf16[394,1536]{1,0:T(8,128)(2,1)} %get-tuple-element.87, bf16[394,768]{1,0:T(8,128)(2,1)} %param.17, f32[394]{0:T(512)S(1)} %fusion.59), kind=kOutput, calls=%fused_computation.9 | convolution fusion | flops 931650048 | bytes 4176424 | tf_op jit(solution)/shard_map/dot_general | solution.py:52
  206.6 2.0 fusion.31
  208.6 1.5 fusion.39
  210.6 1.7 pad_maximum_fusion.2
  213.1 1.7 convolution_convert_fusion.8
  214.8 1.5 collective-permute-done.2
  216.2 1.8 collective-permute-start.3
  218.1 1.7 pad_maximum_fusion.1
  219.7 81.4 %scatter_all.1 = (f32[48,1536]{1,0:T(8,128)S(1)}, f32[48,1536]{1,0:T(8,128)S(1)}, f32[48,1536]{1,0:T(8,128)S(1)}) custom-call(bf16[16,48,1536]{2,1,0:T(8,128)(2,1)S(1)} %bitcast.100, bf16[16,48,1536]{2,1,0:T(8,128)(2,1)S(1)} %bitcast.101, bf16[16,48,1536]{2,1,0:T(8,128)(2,1)} %bitcast.115, bf16[16,48,1536]{2,1,0:T(8,128)(2,1)} %bitcast.105, ...), custom_call_target="tpu_custom_call" | custom-call | tf_op jit(solution)/shard_map/scatter_all/pallas_call | solution.py:246
  301.2 1.1 collective-permute-start.7
  303.0 2.0 collective-permute-done.7
  307.1 3.6 %collective-permute-done.5 = f32[2304]{0:T(1024)S(1)} collective-permute-done((f32[2304]{0:T(1024)S(1)}, f32[2304]{0:T(1024)S(1)}, u32[]{:S(2)}, u32[]{:S(2)}) %collective-permute-start.5) | collective-permute-done | bytes 9248 | tf_op jit(solution)/shard_map/ppermute | solution.py:84
  311.4 3.3 %collective-permute-done.9 = f32[4608]{0:T(1024)S(1)} collective-permute-done((f32[4608]{0:T(1024)S(1)}, f32[4608]{0:T(1024)S(1)}, u32[]{:S(2)}, u32[]{:S(2)}) %collective-permute-start.9) | collective-permute-done | bytes 18464 | tf_op jit(solution)/shard_map/ppermute | solution.py:84
  315.5 3.9 %collective-permute-done.10 = f32[4608]{0:T(1024)S(1)} collective-permute-done((f32[4608]{0:T(1024)S(1)}, f32[4608]{0:T(1024)S(1)}, u32[]{:S(2)}, u32[]{:S(2)}) %collective-permute-start.10) | collective-permute-done | bytes 18464 | tf_op jit(solution)/shard_map/ppermute | solution.py:84
  (188 shorter events, 21.4 us)
Async XLA Ops:
  0.6 74.1 %copy-start.5 = (bf16[394,768]{1,0:T(8,128)(2,1)S(1)}, bf16[394,768]{1,0:T(8,128)(2,1)}, u32[]{:S(2)}) copy-start(bf16[394,768]{1,0:T(8,128)(2,1)} %param.16) | copy-start | bytes 1815556
  0.7 5.5 %copy-start.30 = (bf16[48,1536]{1,0:T(8,128)(2,1)S(1)}, bf16[48,1536]{1,0:T(8,128)(2,1)}, u32[]{:S(2)}) copy-start(bf16[48,1536]{1,0:T(8,128)(2,1)} %param.24) | copy-start | bytes 442372
  0.7 74.1 %copy-start.36 = (f32[768]{0:T(1024)S(1)}, f32[768]{0:T(1024)}, u32[]{:S(2)}) copy-start(f32[768]{0:T(1024)} %param.28) | copy-start | bytes 9220
  0.7 74.1 %copy-start.43 = (f32[768]{0:T(1024)S(1)}, f32[768]{0:T(1024)}, u32[]{:S(2)}) copy-start(f32[768]{0:T(1024)} %param.29) | copy-start | bytes 9220
  1.5 87.5 %collective-permute-start = (f32[2688]{0:T(1024)S(1)}, f32[2688]{0:T(1024)S(1)}, u32[]{:S(2)}, u32[]{:S(2)}) collective-permute-start(f32[2688]{0:T(1024)S(1)} %pad_maximum_fusion.22), channel_id=1, source_target_pairs={{0,1},{1,0},{2,3},{3,2},{4,5},{5,4},{6,7},{7,6},{8,9},{9,8},{10,11... | collective-permute-start | bytes 32264 | tf_op jit(solution)/shard_map/ppermute | solution.py:84
  83.3 5.3 %copy-start.10 = (bf16[2,197,1,6,64]{4,3,2,1,0:T(8,128)(2,1)S(1)}, bf16[2,197,1,6,64]{4,3,2,1,0:T(8,128)(2,1)}, u32[]{:S(2)}) copy-start(bf16[2,197,1,6,64]{4,3,2,1,0:T(8,128)(2,1)} %get-tuple-element.44) | copy-start | bytes 907780
  97.1 1.6 copy-start.12
  97.2 2.9 copy-start.7
  97.2 2.9 copy-start.14
  98.8 3.3 %copy-start.8 = (bf16[2,197,1,6,64]{1,4,3,0,2:T(8,128)(2,1)}, bf16[2,197,1,6,64]{1,4,3,0,2:T(8,128)(2,1)S(1)}, u32[]{:S(2)}) copy-start(bf16[2,197,1,6,64]{1,4,3,0,2:T(8,128)(2,1)S(1)} %copy.85) | copy-start | bytes 907780
  102.1 2.2 copy-start
  102.1 2.2 copy-start.11
  111.9 2.1 copy-start.37
  112.2 3.7 %copy-start.17 = (bf16[394,384]{0,1:T(8,128)(2,1)}, bf16[394,384]{0,1:T(8,128)(2,1)S(1)}, u32[]{:S(2)}) copy-start(bf16[394,384]{0,1:T(8,128)(2,1)S(1)} %reshape.176) | copy-start | bytes 907780
  114.0 2.1 copy-start.33
  114.0 2.1 copy-start.35
  115.8 26.9 %copy-start.1 = (f32[394,768]{1,0:T(8,128)}, f32[394,768]{1,0:T(8,128)S(1)}, u32[]{:S(2)}) copy-start(f32[394,768]{1,0:T(8,128)S(1)} %get-tuple-element.84) | copy-start | bytes 3631108
  115.8 2.3 copy-start.32
  115.9 2.3 copy-start.34
  118.1 2.4 copy-start.25
  118.1 2.4 copy-start.31
  120.5 14.8 %copy-start.27 = (bf16[394,768]{1,0:T(8,128)(2,1)S(1)}, bf16[394,768]{1,0:T(8,128)(2,1)}, u32[]{:S(2)}) copy-start(bf16[394,768]{1,0:T(8,128)(2,1)} %param.17) | copy-start | bytes 1815556
  120.5 14.8 %copy-start.40 = (bf16[16,48,1536]{2,1,0:T(8,128)(2,1)S(1)}, bf16[16,48,1536]{2,1,0:T(8,128)(2,1)}, u32[]{:S(2)}) copy-start(bf16[16,48,1536]{2,1,0:T(8,128)(2,1)} %get-tuple-element.28) | copy-start | bytes 7077892
  137.1 2.1 copy-start.38
  141.1 1.6 copy-start.51
  143.3 1.4 copy-start.3
  143.4 2.5 copy-start.23
  153.6 6.5 %slice-start = ((s8[4915200]{0:T(1024)(128)(4,1)}), s8[4194304]{0:T(1024)(128)(4,1)S(1)}, s32[]{:S(2)}) async-start(s8[4915200]{0:T(1024)(128)(4,1)} %bitcast.103), calls=%async_computation | async-start | bytes 8388608
  153.9 4.2 %copy-start.15 = (bf16[2,197,1,6,64]{1,4,3,0,2:T(8,128)(2,1)S(1)}, bf16[2,197,1,6,64]{1,4,3,0,2:T(8,128)(2,1)}, u32[]{:S(2)}) copy-start(bf16[2,197,1,6,64]{1,4,3,0,2:T(8,128)(2,1)} %copy.86) | copy-start | bytes 907780
  153.9 4.2 %copy-start.16 = (bf16[2,197,1,6,64]{1,4,3,0,2:T(8,128)(2,1)S(1)}, bf16[2,197,1,6,64]{1,4,3,0,2:T(8,128)(2,1)}, u32[]{:S(2)}) copy-start(bf16[2,197,1,6,64]{1,4,3,0,2:T(8,128)(2,1)} %copy.87) | copy-start | bytes 907780
  153.9 6.1 %slice-start.1 = ((s8[4915200]{0:T(1024)(128)(4,1)}), s8[720896]{0:T(1024)(128)(4,1)S(1)}, s32[]{:S(2)}) async-start(s8[4915200]{0:T(1024)(128)(4,1)} %bitcast.103), calls=%async_computation.1 | async-start | bytes 1441792
  160.1 1.2 copy-start.26
  160.1 1.5 copy-start.52
  161.6 2.8 copy-start.18
  161.6 2.8 copy-start.24
  164.4 1.5 copy-start.48
  175.8 4.2 %copy-start.22 = (bf16[394,1152]{0,1:T(8,128)(2,1)S(1)}, bf16[394,1152]{0,1:T(8,128)(2,1)}, u32[]{:S(2)}) copy-start(bf16[394,1152]{0,1:T(8,128)(2,1)} %reshape.182) | copy-start | bytes 2723332
  180.0 2.7 copy-start.28
  180.0 2.7 copy-start.45
  182.8 3.0 copy-start.41
  185.7 2.8 copy-start.6
  188.0 113.2 %collective-permute-start.6 = (f32[4608]{0:T(1024)S(1)}, f32[4608]{0:T(1024)S(1)}, u32[]{:S(2)}, u32[]{:S(2)}) collective-permute-start(f32[4608]{0:T(1024)S(1)} %get-tuple-element.73), channel_id=1, source_target_pairs={{0,1},{1,0},{2,3},{3,2},{4,5},{5,4},{6,7},{7,6},{8,9},{9,8},{10,11... | collective-permute-start | bytes 55304 | tf_op jit(solution)/shard_map/ppermute | solution.py:84
  194.9 4.1 %copy-start.21 = (bf16[394,1152]{0,1:T(8,128)(2,1)S(1)}, bf16[394,1152]{0,1:T(8,128)(2,1)}, u32[]{:S(2)}) copy-start(bf16[394,1152]{0,1:T(8,128)(2,1)} %reshape.183) | copy-start | bytes 2723332
  194.9 4.1 %copy-start.42 = (bf16[16,48,1152]{2,1,0:T(8,128)(2,1)S(1)}, bf16[16,48,1152]{2,1,0:T(8,128)(2,1)}, u32[]{:S(2)}) copy-start(bf16[16,48,1152]{2,1,0:T(8,128)(2,1)} %get-tuple-element.25) | copy-start | bytes 5308420
  194.9 4.1 %copy-start.50 = (f32[394,768]{1,0:T(8,128)S(1)}, f32[394,768]{1,0:T(8,128)}, u32[]{:S(2)}) copy-start(f32[394,768]{1,0:T(8,128)} %fusion.91) | copy-start | bytes 3631108
  201.8 10.7 %collective-permute-start.1 = (f32[2304]{0:T(1024)S(1)}, f32[2304]{0:T(1024)S(1)}, u32[]{:S(2)}, u32[]{:S(2)}) collective-permute-start(f32[2304]{0:T(1024)S(1)} %pad_maximum_fusion.18), channel_id=1, source_target_pairs={{0,1},{1,0},{2,3},{3,2},{4,5},{5,4},{6,7},{7,6},{8,9},{9,8},{10,11... | collective-permute-start | bytes 27656 | tf_op jit(solution)/shard_map/ppermute | solution.py:84
  201.9 4.6 %copy-start.2 = (f32[394,768]{1,0:T(8,128)S(1)}, f32[394,768]{1,0:T(8,128)}, u32[]{:S(2)}) copy-start(f32[394,768]{1,0:T(8,128)} %copy-done.1) | copy-start | bytes 3631108
  201.9 4.6 %copy-start.39 = (bf16[16,48,1536]{2,1,0:T(8,128)(2,1)S(1)}, bf16[16,48,1536]{2,1,0:T(8,128)(2,1)}, u32[]{:S(2)}) copy-start(bf16[16,48,1536]{2,1,0:T(8,128)(2,1)} %get-tuple-element.29) | copy-start | bytes 7077892
  201.9 4.6 %copy-start.44 = (f32[768]{0:T(1024)S(1)}, f32[768]{0:T(1024)}, u32[]{:S(2)}) copy-start(f32[768]{0:T(1024)} %param.27) | copy-start | bytes 9220
  201.9 4.6 %copy-start.46 = (f32[394,768]{1,0:T(8,128)S(1)}, f32[394,768]{1,0:T(8,128)}, u32[]{:S(2)}) copy-start(f32[394,768]{1,0:T(8,128)} %fusion.90) | copy-start | bytes 3631108
  201.9 4.6 %copy-start.49 = (bf16[394,1536]{1,0:T(8,128)(2,1)S(1)}, bf16[394,1536]{1,0:T(8,128)(2,1)}, u32[]{:S(2)}) copy-start(bf16[394,1536]{1,0:T(8,128)(2,1)} %get-tuple-element.87) | copy-start | bytes 3631108
  206.5 2.0 copy-start.4
  206.6 2.0 copy-start.20
  208.6 1.6 copy-start.13
  208.6 2.0 copy-start.29
  210.6 2.4 copy-start.19
  212.5 3.8 %collective-permute-start.2 = (f32[2304]{0:T(1024)S(1)}, f32[2304]{0:T(1024)S(1)}, u32[]{:S(2)}, u32[]{:S(2)}) collective-permute-start(f32[2304]{0:T(1024)S(1)} %fusion.57), channel_id=1, source_target_pairs={{0,2},{2,0},{4,6},{6,4},{8,10},{10,8},{12,14},{14,12},{16,18},{18,... | collective-permute-start | bytes 27656 | tf_op jit(solution)/shard_map/ppermute | solution.py:84
  216.2 86.1 %collective-permute-start.3 = (f32[2304]{0:T(1024)S(1)}, f32[2304]{0:T(1024)S(1)}, u32[]{:S(2)}, u32[]{:S(2)}) collective-permute-start(f32[2304]{0:T(1024)S(1)} %add.203), channel_id=1, source_target_pairs={{0,4},{2,6},{4,0},{6,2},{8,12},{10,14},{12,8},{14,10},{16,20},{18,... | collective-permute-start | bytes 27656 | tf_op jit(solution)/shard_map/ppermute | solution.py:84
  301.2 3.8 %collective-permute-start.7 = (f32[4608]{0:T(1024)S(1)}, f32[4608]{0:T(1024)S(1)}, u32[]{:S(2)}, u32[]{:S(2)}) collective-permute-start(f32[4608]{0:T(1024)S(1)} %add.207), channel_id=1, source_target_pairs={{0,2},{2,0},{4,6},{6,4},{8,10},{10,8},{12,14},{14,12},{16,18},{18,... | collective-permute-start | bytes 55304 | tf_op jit(solution)/shard_map/ppermute | solution.py:84
  302.3 3.7 %collective-permute-start.4 = (f32[2304]{0:T(1024)S(1)}, f32[2304]{0:T(1024)S(1)}, u32[]{:S(2)}, u32[]{:S(2)}) collective-permute-start(f32[2304]{0:T(1024)S(1)} %add.204), channel_id=1, source_target_pairs={{0,8},{2,10},{4,12},{6,14},{8,0},{10,2},{12,4},{14,6},{16,24},{18,... | collective-permute-start | bytes 27656 | tf_op jit(solution)/shard_map/ppermute | solution.py:84
  305.0 5.7 %collective-permute-start.8 = (f32[4608]{0:T(1024)S(1)}, f32[4608]{0:T(1024)S(1)}, u32[]{:S(2)}, u32[]{:S(2)}) collective-permute-start(f32[4608]{0:T(1024)S(1)} %add.208), channel_id=1, source_target_pairs={{0,4},{2,6},{4,0},{6,2},{8,12},{10,14},{12,8},{14,10},{16,20},{18,... | collective-permute-start | bytes 55304 | tf_op jit(solution)/shard_map/ppermute | solution.py:84
  306.0 4.7 %collective-permute-start.5 = (f32[2304]{0:T(1024)S(1)}, f32[2304]{0:T(1024)S(1)}, u32[]{:S(2)}, u32[]{:S(2)}) collective-permute-start(f32[2304]{0:T(1024)S(1)} %add.205), channel_id=1, source_target_pairs={{0,16},{2,18},{4,20},{6,22},{8,24},{10,26},{12,28},{14,30},{16,0},... | collective-permute-start | bytes 27656 | tf_op jit(solution)/shard_map/ppermute | solution.py:84
  310.7 3.9 %collective-permute-start.9 = (f32[4608]{0:T(1024)S(1)}, f32[4608]{0:T(1024)S(1)}, u32[]{:S(2)}, u32[]{:S(2)}) collective-permute-start(f32[4608]{0:T(1024)S(1)} %add.209), channel_id=1, source_target_pairs={{0,8},{2,10},{4,12},{6,14},{8,0},{10,2},{12,4},{14,6},{16,24},{18,... | collective-permute-start | bytes 55304 | tf_op jit(solution)/shard_map/ppermute | solution.py:84
  314.7 4.7 %collective-permute-start.10 = (f32[4608]{0:T(1024)S(1)}, f32[4608]{0:T(1024)S(1)}, u32[]{:S(2)}, u32[]{:S(2)}) collective-permute-start(f32[4608]{0:T(1024)S(1)} %add.210), channel_id=1, source_target_pairs={{0,16},{2,18},{4,20},{6,22},{8,24},{10,26},{12,28},{14,30},{16,0},... | collective-permute-start | bytes 55304 | tf_op jit(solution)/shard_map/ppermute | solution.py:84
  (2 other events, 2.2 us)
where the time goes:
time: 320 us; the launch traced here: 322 us
  Pallas kernels  148 us (46%)
  matrix products  81.9 us (26%)
  local copies, waits for them, and re-layouts  54.3 us (17%)
  other arithmetic  14.9 us (5%)
  waiting for transfers between devices  14.8 us (5%)
  starting transfers between devices  5.79 us (2%)
    pallas_call x1, Pallas kernels, scatter_all(): pl.pallas_call(functools.partial(scatter_kernel, count, [order_of(f) for...  81.4 us
    pallas_call x1, Pallas kernels, gather_all(): pl.pallas_call(functools.partial(gather_kernel, count, [order_of(f)[::-1]...  66.5 us
    dot_general x8, matrix products, dot_nn(): lax.dot_general(left, right, (((1,), (0,)), ((), ())), preferred_element_...  30.4 us
    dot_general x8, matrix products, dot_tn(): lax.dot_general(left, right, (((0,), (0,)), ((), ())), preferred_element_...  21.8 us
    dot_general x8, matrix products, dot_nt(): lax.dot_general(left, right, (((1,), (1,)), ((), ())), preferred_element_...  17.3 us
    unnamed x122, local copies, waits for them, and re-layouts  14.9 us
    ppermute x11, waiting for transfers between devices, swap(): return lax.ppermute(value, axis, [(i, i ^ 1 << bit) for i in range(size)])  14.8 us
  transfers between devices with their start and end apart: 11, of which 6 were waited for; matrix products, arithmetic and copies ran while one was open for 15% of the time, Pallas kernels for 46%

commit v1 on v0

--- a/solution.py
+++ b/solution.py
@@ -187,9 +187,11 @@
 
 def scatter_kernel(count, orders, *refs):
     k = len(orders)
-    own, oth, out = refs[:k], refs[k : 2 * k], refs[2 * k : 3 * k]
-    from_twin, sent, came = refs[3 * k : 4 * k], refs[4 * k : 5 * k], refs[5 * k : 6 * k]
-    ring, pair = refs[6 * k : 6 * k + 2], refs[6 * k + 2 : 6 * k + 4]
+    own, oth, refs = refs[:k], refs[k : 2 * k], refs[2 * k :]
+    vec_own, vec_oth, refs = refs[0], refs[1], refs[2:]
+    out, vec_out, refs = refs[:k], refs[k], refs[k + 1 :]
+    from_twin, sent, came, refs = refs[:k], refs[k : 2 * k], refs[2 * k : 3 * k], refs[3 * k :]
+    vec_sent, vec_came, ring, pair, line = refs[0], refs[1], refs[2:4], refs[4:6], refs[6:8]
     size = 1 << count
     bits, near, twin = enter(count)
     copies = []
@@ -200,13 +202,26 @@
             return [0]
         return [r for r in range(size) if r & done == 0 and (r >> orders[c][step]) & 1]
 
+    copies.append(remote(vec_oth, vec_came.at[0], line, 0, twin))
+    copies[0].start()
     for step in range(count + 1):
         for c in range(k):
             for rel in stage(c, step):
                 copy = remote(oth[c].at[place(bits, rel)], from_twin[c].at[rel], pair, c * size + rel, twin)
                 copy.start()
                 copies.append(copy)
+    vector = vec_own[...]
     for step in range(count + 1):
+        slot = vec_came.at[step]
+        remote(slot, slot, line, step, twin).wait_recv()
+        vector = vector + vec_came[step]
+        if step == count:
+            vec_out[...] = vector
+        else:
+            vec_sent[step] = vector
+            copy = remote(vec_sent.at[step], vec_came.at[step + 1], line, step + 1, near[step])
+            copy.start()
+            copies.append(copy)
         for c in range(k):
             for rel in stage(c, step):
                 slot = from_twin[c].at[rel]
@@ -230,7 +245,7 @@
         copy.wait_send()
 
 
-def scatter_all(owns, others, firsts):
+def scatter_all(owns, others, firsts, split_own, split_other, whole):
     size = lax.axis_size("fsdp")
     rows = owns[0].shape[0] // size
     owns, others = [o.astype(BF) for o in owns], [o.astype(BF) for o in others]
@@ -240,21 +255,32 @@
                 o.astype(F32) + swap(t, "tp", 0).astype(F32), "fsdp", scatter_dimension=0, tiled=True
             )
             for o, t in zip(owns, others)
-        ]
+        ], all_sum(split_own, split_other, whole)
     count, k = bits_of("fsdp"), len(owns)
     blocks = [(size, rows, o.shape[1]) for o in owns]
-    return pl.pallas_call(
+    vec_own, vec_oth = jnp.concatenate(split_own + whole), jnp.concatenate(split_other + whole)
+    length = vec_own.shape[0]
+    lines = -(-length // 1024) * 8
+    vec_own, vec_oth = [
+        jnp.pad(v, (0, lines * 128 - length)).reshape(lines, 128) for v in (vec_own, vec_oth)
+    ]
+    in_vmem = pl.BlockSpec(memory_space=pltpu.VMEM)
+    *sums, total = pl.pallas_call(
         functools.partial(scatter_kernel, count, [order_of(f) for f in firsts]),
-        out_shape=[jax.ShapeDtypeStruct(b[1:], F32) for b in blocks],
-        in_specs=[pl.BlockSpec(memory_space=pltpu.VMEM)] * k + [pl.BlockSpec(memory_space=pl.ANY)] * k,
-        out_specs=[pl.BlockSpec(memory_space=pltpu.VMEM)] * k,
+        out_shape=[jax.ShapeDtypeStruct(b[1:], F32) for b in blocks]
+        + [jax.ShapeDtypeStruct((lines, 128), F32)],
+        in_specs=[in_vmem] * k + [pl.BlockSpec(memory_space=pl.ANY)] * k + [in_vmem] * 2,
+        out_specs=[in_vmem] * (k + 1),
         scratch_shapes=[pltpu.VMEM(b, BF) for b in blocks] * 3
-        + [pltpu.SemaphoreType.DMA((k * size,))] * 4,
+        + [pltpu.VMEM((count, lines, 128), F32), pltpu.VMEM((count + 1, lines, 128), F32)]
+        + [pltpu.SemaphoreType.DMA((k * size,))] * 4
+        + [pltpu.SemaphoreType.DMA((count + 1,))] * 2,
         compiler_params=pltpu.CompilerParams(
             collective_id=1, has_side_effects=True, vmem_limit_bytes=48 * 1024 * 1024
         ),
         name="scatter_all",
-    )(*[o.reshape(b) for o, b in zip(owns, blocks)], *[o.reshape(b) for o, b in zip(others, blocks)])
+    )(*[o.reshape(b) for o, b in zip(owns, blocks)], *[o.reshape(b) for o, b in zip(others, blocks)], vec_own, vec_oth)
+    return sums, cut_up(total.reshape(-1), split_own + whole)
 
 
 def all_sum(split_own, split_other, whole):
@@ -266,8 +292,12 @@
             total = total + swap(total, "fsdp", bit)
     else:
         total = lax.psum(total, "fsdp")
+    return cut_up(total, split_own + whole)
+
+
+def cut_up(total, pieces):
     parts, at = [], 0
-    for piece in split_own + whole:
+    for piece in pieces:
         parts.append(total[at : at + piece.shape[0]])
         at += piece.shape[0]
     return parts
@@ -337,11 +367,6 @@
     dn2 = dot_nt(dpo, wu_own) + dot_nt(dpt, wu_oth)
     dmid = doutf + norm_back(dn2, xh2, rs2, gain_two)
     dmid_b = dmid.astype(BF)
-    part_bup, sum_bdown, sum_gain2, sum_shift2, sum_bout = all_sum(
-        [jnp.sum(dpre_own, axis=0)],
-        [jnp.sum(dpre_oth, axis=0)],
-        [jnp.sum(doutf, axis=0), jnp.sum(dn2 * xh2, axis=0), jnp.sum(dn2, axis=0), jnp.sum(dmid, axis=0)],
-    )
     shape4 = (images, SEQ, heads, HEAD_DIM)
     datt = jnp.concatenate(
         [
@@ -358,12 +383,7 @@
     d_oth = d5[:, :, :, heads:].reshape(rows, cut)
     dn1 = dot_nt(d_own, qkv_own) + dot_nt(d_oth, qkv_oth)
     grad_tokens = dmid + norm_back(dn1, xh1, rs1, gain_one)
-    part_bq, part_bv, sum_gain1, sum_shift1 = all_sum(
-        [g_bq[:head_width], g_bv[:head_width]],
-        [g_bq[head_width:], g_bv[head_width:]],
-        [jnp.sum(dn1 * xh1, axis=0), jnp.sum(dn1, axis=0)],
-    )
-    s_heads, s_up, s_down = scatter_all(
+    (s_heads, s_up, s_down), vectors = scatter_all(
         [
             jnp.concatenate([dot_tn(h1, d_own).astype(BF), dot_tn(dmid_b, att_own).astype(BF)], axis=1),
             dot_tn(h2, dpo),
@@ -375,7 +395,18 @@
             dot_tn(dout, act_oth),
         ],
         [(0, 1), (1, 0), (2, 0)],
-    )
+        [jnp.sum(dpre_own, axis=0), g_bq[:head_width], g_bv[:head_width]],
+        [jnp.sum(dpre_oth, axis=0), g_bq[head_width:], g_bv[head_width:]],
+        [
+            jnp.sum(doutf, axis=0),
+            jnp.sum(dn2 * xh2, axis=0),
+            jnp.sum(dn2, axis=0),
+            jnp.sum(dmid, axis=0),
+            jnp.sum(dn1 * xh1, axis=0),
+            jnp.sum(dn1, axis=0),
+        ],
+    )
+    part_bup, part_bq, part_bv, sum_bdown, sum_gain2, sum_shift2, sum_bout, sum_gain1, sum_shift1 = vectors
     s_qkv, s_out = s_heads[:, :cut], s_heads[:, cut:]
     return (
         block_out,

time: 320 us -> 287 us (0.90); the launches traced: 322 us -> 283 us
  matrix products: 81.9 us -> 64.1 us
  waiting for transfers between devices: 14.8 us -> 0.01 us
  starting transfers between devices: 5.79 us -> 0.45 us
    ppermute x11 -> x1, waiting for transfers between devices: 14.8 us -> 0.01 us  [swap(): return lax.ppermute(value, axis, [(i, i ^ 1 << bit) for i in range(size)])]
    dot_general x8, matrix products: 30.4 us -> 18.4 us  [dot_nn(): lax.dot_general(left, right, (((1,), (0,)), ((), ())), preferred_element_...]
    ppermute x11 -> x1, starting transfers between devices: 5.79 us -> 0.45 us  [swap(): return lax.ppermute(value, axis, [(i, i ^ 1 << bit) for i in range(size)])]
    unnamed x122 -> x133, local copies, waits for them, and re-layouts: 14.9 us -> 15.1 us
  transfers between devices with their start and end apart: 11 -> 1, of which waited for: 6 -> 0; matrix products, arithmetic and copies ran while one was open for 15% -> 7% of each run, Pallas kernels for 46% -> 23%
where the time goes in v1:
time: 287 us; the launch traced here: 283 us
  Pallas kernels  150 us (52%)
  matrix products  64.1 us (22%)
  local copies, waits for them, and re-layouts  52.9 us (18%)
  other arithmetic  13.3 us (5%)
    pallas_call x1, Pallas kernels, scatter_all(): pl.pallas_call(functools.partial(scatter_kernel, count, [order_of(f) for...  83.4 us
    pallas_call x1, Pallas kernels, gather_all(): pl.pallas_call(functools.partial(gather_kernel, count, [order_of(f)[::-1]...  66.5 us
    dot_general x8, matrix products, dot_tn(): lax.dot_general(left, right, (((0,), (0,)), ((), ())), preferred_element_...  18.7 us
    dot_general x8, matrix products, dot_nn(): lax.dot_general(left, right, (((1,), (0,)), ((), ())), preferred_element_...  18.4 us
    dot_general x8, matrix products, dot_nt(): lax.dot_general(left, right, (((1,), (1,)), ((), ())), preferred_element_...  15.3 us
    unnamed x133, local copies, waits for them, and re-layouts  15.1 us
  transfers between devices with their start and end apart: 1, of which 0 were waited for; matrix products, arithmetic and copies ran while one was open for 7% of the time, Pallas kernels for 23%

profile of v1, /device:TPU:0, one launch (start us, length us, event | category | flops | bytes accessed | tf_op | source)
XLA Modules:
  0.0 283.3 jit_solution(2671079530798396984)
XLA Ops:
  0.7 0.8 pad_maximum_fusion.18
  2.0 0.7 pad_maximum_fusion.19
  2.7 0.8 slice_bitcast_fusion.6
  3.5 1.2 convert_reduce_fusion
  4.7 1.4 fusion.41
  6.2 1.5 pad_maximum_fusion.16.refs_1_
  8.3 66.5 %gather_all.1 = (bf16[16,48,1152]{2,1,0:T(8,128)(2,1)}, bf16[16,48,1920]{2,1,0:T(8,128)(2,1)}, bf16[16,48,1536]{2,1,0:T(8,128)(2,1)}, bf16[16,48,1152]{2,1,0:T(8...) custom-call(bf16[48,1152]{1,0:T(8,128)(2,1)} %pad_maximum_fusion.17.refs_0_, ...), custom_call_target="tpu_custom_call" | custom-call | tf_op jit(solution)/shard_map/gather_all/pallas_call | solution.py:175
  74.8 3.5 %fusion.1 = bf16[394,1152]{1,0:T(8,128)(2,1)} fusion(bf16[768,1152]{1,0:T(8,128)(2,1)} %bitcast.160, f32[1152]{0:T(1024)S(1)} %pad_maximum_fusion.19, bf16[394,768]{1,0:T(8,128)(2,1)S(1)} %copy-done.5, f32[768]{0:T(1024)S(1)} %copy-done.46, f32[768]{0:T(1024)S(1)} %copy-done.39, f32[394]{0:T(512)S(1)} %add_rsqrt_fusion.1, f32[394]{0:T(512)S(1)} %broadcast_multiply_fusion.5), kind=kOutput, calls=%fused_computation.16 | convolution fusion | flops 699895296 | bytes 3296336 | tf_op jit(solution)/shard_map/dot_general | solution.py:44
  78.3 3.2 %reshape.210 = bf16[2,197,3,6,64]{4,3,2,1,0:T(8,128)(2,1)S(1)} reshape(bf16[394,1152]{1,0:T(8,128)(2,1)} %fusion.1) | data formatting | bytes 1815552 | tf_op jit(solution)/shard_map/reshape | solution.py:348
  81.5 1.6 fusion.77
  83.9 2.3 copy.86
  86.2 2.3 copy.84
  88.9 3.5 %add_convert_fusion = bf16[394,1152]{1,0:T(8,128)(2,1)} fusion(f32[1152]{0:T(1024)S(1)} %slice.203, bf16[768,1152]{1,0:T(8,128)(2,1)} %bitcast.158, bf16[394,768]{1,0:T(8,128)(2,1)S(1)} %copy-done.5, f32[768]{0:T(1024)S(1)} %copy-done.46, f32[768]{0:T(1024)S(1)} %copy-done.39, f32[394]{0:T(512)S(1)} %add_rsqrt_fusion.1, f32[394]{0:T(512)S(1)} %broadcast_multiply_fusion.5), kind=kOutput, calls=%fused_computation.40 | convolution fusion | flops 699895296 | bytes 3296336 | tf_op jit(solution)/shard_map/dot_general | solution.py:44
  92.5 3.0 %reshape.211 = bf16[2,197,3,6,64]{4,3,2,1,0:T(8,128)(2,1)S(1)} reshape(bf16[394,1152]{1,0:T(8,128)(2,1)} %add_convert_fusion) | data formatting | bytes 1815552 | tf_op jit(solution)/shard_map/reshape | solution.py:349
  95.5 1.6 fusion.78
  97.1 1.6 copy.85
  99.2 1.1 multiply_reduce_fusion
  100.3 0.9 exponential_reduce_fusion
  101.2 1.3 copy-done
  103.0 3.6 %fusion.32 = bf16[2,197,12,64]{1,3,2,0:T(8,128)(2,1)S(1)} fusion(bf16[2,197,6,64]{1,3,2,0:T(8,128)(2,1)S(1)} %bitcast.130, bf16[2,197,6,64]{1,3,2,0:T(8,128)(2,1)S(1)} %bitcast.128, f32[2,12,197,197]{2,3,1,0:T(8,128)} %copy-done, f32[2,12,197]{2,1,0:T(8,128)S(1)} %log_add_fusion), kind=kOutput, calls=%fused_computation.71 | convolution fusion | flops 122620680 | bytes 4954944 | tf_op jit(solution)/shard_map/bhqk,bkhe->bqhe/dot_general | solution.py:64
  107.1 1.0 reshape.190
  108.8 1.9 fusion.51
  110.7 1.8 fusion.83
  113.1 1.7 copy-done.35
  114.8 2.4 multiply_convert_fusion.2
  117.2 2.9 %multiply_convert_fusion.1 = (bf16[394,1536]{1,0:T(8,128)(2,1)}, f32[394,1536]{1,0:T(8,128)S(1)}) fusion(f32[1536]{0:T(1024)S(1)} %slice.215, bf16[394,768]{1,0:T(8,128)(2,1)S(1)} %add_convert_fusion.1, bf16[768,1920]{1,0:T(8,128)(2,1)S(1)} %bitcast.146), kind=kOutput, calls=%fused_computation.26 | convolution fusion | flops 933193728 | bytes 6612992 | tf_op jit(solution)/shard_map/dot_general | solution.py:44
  120.0 1.8 fusion.85
  121.9 1.1 fusion.15
  123.0 1.0 copy-done.41
  124.0 1.9 fusion.84
  125.9 1.6 multiply_reduce_fusion.2
  128.2 1.2 convolution_convert_fusion.10
  129.4 1.2 convolution_convert_fusion.9
  130.6 2.3 reshape.208
  132.9 1.5 copy.57
  134.4 2.3 reshape.209
  136.8 1.5 copy.58
  138.6 3.8 %bitcast_reduce_fusion = (f32[12,64]{1,0:T(8,128)S(1)}, bf16[2,12,64,197]{3,2,1,0:T(8,128)(2,1)S(1)}) fusion(f32[2,12,197,197]{2,3,1,0:T(8,128)} %copy-done, f32[2,12,197]{2,1,0:T(8,128)S(1)} %log_add_fusion, bf16[2,197,6,64]{1,3,2,0:T(8,128)(2,1)S(1)} %copy.58, bf16[2,197,6,64]{1,3,2,0:T(8,128)(2,1)S(1)} %copy.57), kind=kOutput, calls=%fused_computation.44 | convolution fusion | flops 122922504 | bytes 4958016 | tf_op jit(solution)/shard_map/bhqk,bqhe->bkhe/dot_general | solution.py:74
  142.4 1.6 multiply_convert_fusion
  144.1 0.7 bitcast_reduce_fusion.1
  145.2 0.9 fusion.33
  146.7 2.9 %convolution_convert_fusion.3 = bf16[768,1536]{1,0:T(8,128)(2,1)} fusion(bf16[394,768]{1,0:T(8,128)(2,1)S(1)} %copy-done.26, bf16[394,1536]{1,0:T(8,128)(2,1)S(1)} %copy-done.54), kind=kOutput, calls=%fused_computation.10 | convolution fusion | flops 930742272 | bytes 4174848 | tf_op jit(solution)/shard_map/dot_general | solution.py:52
  149.6 1.5 convolution_convert_fusion.7
  151.0 1.4 convolution_convert_fusion.5
  152.5 1.4 convolution_convert_fusion.8
  154.6 1.2 fusion.79
  155.8 2.2 copy.63
  158.1 4.1 %reshape.198 = bf16[394,1152]{0,1:T(8,128)(2,1)} reshape(bf16[2,197,3,6,64]{1,0,4,3,2:T(2,128)(2,1)} %copy.63) | data formatting | bytes 1815552 | tf_op jit(solution)/shard_map/reshape | solution.py:382
  162.2 4.1 %fusion.87 = f32[394,768]{1,0:T(8,128)} fusion(bf16[394,1152]{0,1:T(8,128)(2,1)} %reshape.198, bf16[768,1152]{1,0:T(8,128)(2,1)} %bitcast.161), kind=kOutput, calls=%fused_computation.186 | convolution fusion | flops 697171968 | bytes 3887616 | tf_op jit(solution)/shard_map/dot_general | solution.py:48
  166.3 2.8 convolution_convert_fusion.1
  169.4 3.5 %copy.64 = bf16[2,197,3,6,64]{1,0,4,3,2:T(2,128)(2,1)} copy(bf16[2,197,3,6,64]{1,4,3,0,2:T(8,128)(2,1)} %get-tuple-element.51) | data formatting | bytes 1815552 | tf_op jit(solution)/shard_map/slice | solution.py:383
  172.9 3.9 %reshape.199 = bf16[394,1152]{0,1:T(8,128)(2,1)} reshape(bf16[2,197,3,6,64]{1,0,4,3,2:T(2,128)(2,1)} %copy.64) | data formatting | bytes 1815552 | tf_op jit(solution)/shard_map/reshape | solution.py:383
  176.8 2.9 %convolution_convert_fusion = bf16[768,1152]{1,0:T(8,128)(2,1)S(1)} fusion(bf16[394,1152]{0,1:T(8,128)(2,1)} %reshape.199, bf16[394,768]{1,0:T(8,128)(2,1)S(1)} %copy-done.5, f32[768]{0:T(1024)S(1)} %copy-done.46, f32[768]{0:T(1024)S(1)} %copy-done.39, f32[394]{0:T(512)S(1)} %add_rsqrt_fusion.1, f32[394]{0:T(512)S(1)} %broadcast_multiply_fusion.5), kind=kOutput, calls=%fused_computation.7 | convolution fusion | flops 699872256 | bytes 3291728 | tf_op jit(solution)/shard_map/dot_general | solution.py:52
  179.8 1.6 fusion.40
  181.6 3.0 %convolution_convert_fusion.2 = bf16[768,1536]{1,0:T(8,128)(2,1)} fusion(bf16[394,1536]{1,0:T(8,128)(2,1)S(1)} %copy-done.51, bf16[394,768]{1,0:T(8,128)(2,1)S(1)} %copy-done.30, f32[394]{0:T(512)S(1)} %fusion.58), kind=kOutput, calls=%fused_computation.9 | convolution fusion | flops 931650048 | bytes 4176424 | tf_op jit(solution)/shard_map/dot_general | solution.py:52
  184.6 3.0 %convolution_convert_fusion.4 = bf16[768,1536]{1,0:T(8,128)(2,1)} fusion(bf16[394,1536]{1,0:T(8,128)(2,1)S(1)} %copy-done.48, bf16[394,768]{1,0:T(8,128)(2,1)S(1)} %copy-done.30, f32[394]{0:T(512)S(1)} %fusion.58), kind=kOutput, calls=%fused_computation.11 | convolution fusion | flops 931650048 | bytes 4176424 | tf_op jit(solution)/shard_map/dot_general | solution.py:52
  187.5 1.7 pad_maximum_fusion.2
  190.2 83.4 %scatter_all.1 = (f32[48,1536]{1,0:T(8,128)S(1)}, f32[48,1536]{1,0:T(8,128)S(1)}, f32[48,1536]{1,0:T(8,128)S(1)}, f32[56,128]{1,0:T(8,128)S(1)}) custom-call(bf16[16,48,1536]{2,1,0:T(8,128)(2,1)S(1)} %bitcast.122, bf16[16,48,1536]{2,1,0:T(8,128)(2,1)S(1)} %bitcast.123, bf16[16,48,1536]{2,1,0:T(8,128)(2,1)} %bitcast.138, bf16[16,48,1536]{2,1,0:T(8,128)(2,1)} %bitcast.127, ...), custom_call_target="tpu_custom_call" | custom-call | tf_op jit(solution)/shard_map/scatter_all/pallas_call | solution.py:268
  275.4 1.1 fusion.86
  277.5 2.0 fusion.31
  279.5 0.7 pad_maximum_fusion.15
  280.2 1.5 fusion.39
  281.7 0.7 copy.109
  282.4 0.7 copy.110
  (169 shorter events, 11.0 us)
Async XLA Ops:
  0.6 74.1 %copy-start.5 = (bf16[394,768]{1,0:T(8,128)(2,1)S(1)}, bf16[394,768]{1,0:T(8,128)(2,1)}, u32[]{:S(2)}) copy-start(bf16[394,768]{1,0:T(8,128)(2,1)} %param.16) | copy-start | bytes 1815556
  0.7 5.5 %copy-start.33 = (bf16[48,1536]{1,0:T(8,128)(2,1)S(1)}, bf16[48,1536]{1,0:T(8,128)(2,1)}, u32[]{:S(2)}) copy-start(bf16[48,1536]{1,0:T(8,128)(2,1)} %param.24) | copy-start | bytes 442372
  0.7 74.1 %copy-start.39 = (f32[768]{0:T(1024)S(1)}, f32[768]{0:T(1024)}, u32[]{:S(2)}) copy-start(f32[768]{0:T(1024)} %param.28) | copy-start | bytes 9220
  0.7 74.1 %copy-start.46 = (f32[768]{0:T(1024)S(1)}, f32[768]{0:T(1024)}, u32[]{:S(2)}) copy-start(f32[768]{0:T(1024)} %param.29) | copy-start | bytes 9220
  1.5 87.4 %collective-permute-start = (f32[2688]{0:T(1024)S(1)}, f32[2688]{0:T(1024)S(1)}, u32[]{:S(2)}, u32[]{:S(2)}) collective-permute-start(f32[2688]{0:T(1024)S(1)} %pad_maximum_fusion.18), channel_id=1, source_target_pairs={{0,1},{1,0},{2,3},{3,2},{4,5},{5,4},{6,7},{7,6},{8,9},{9,8},{10,11... | collective-permute-start | bytes 32264 | tf_op jit(solution)/shard_map/ppermute | solution.py:84
  83.2 5.3 %copy-start.12 = (bf16[2,197,1,6,64]{4,3,2,1,0:T(8,128)(2,1)S(1)}, bf16[2,197,1,6,64]{4,3,2,1,0:T(8,128)(2,1)}, u32[]{:S(2)}) copy-start(bf16[2,197,1,6,64]{4,3,2,1,0:T(8,128)(2,1)} %get-tuple-element.46) | copy-start | bytes 907780
  97.1 1.6 copy-start.14
  97.1 2.1 copy-start.8
  97.1 2.1 copy-start.16
  98.7 1.6 copy-start.10
  99.2 1.1 copy-start.18
  100.3 2.2 copy-start
  100.3 2.2 copy-start.13
  103.0 3.6 %copy-start.6 = (bf16[2,197,1,6,64]{1,4,3,0,2:T(8,128)(2,1)}, bf16[2,197,1,6,64]{1,4,3,0,2:T(8,128)(2,1)S(1)}, u32[]{:S(2)}) copy-start(bf16[2,197,1,6,64]{1,4,3,0,2:T(8,128)(2,1)S(1)} %copy.83) | copy-start | bytes 907780
  108.5 2.1 copy-start.40
  108.8 3.7 %copy-start.20 = (bf16[394,384]{0,1:T(8,128)(2,1)}, bf16[394,384]{0,1:T(8,128)(2,1)S(1)}, u32[]{:S(2)}) copy-start(bf16[394,384]{0,1:T(8,128)(2,1)S(1)} %reshape.192) | copy-start | bytes 907780
  110.7 2.1 copy-start.36
  110.7 2.1 copy-start.38
  112.5 15.0 %copy-start.1 = (f32[394,768]{1,0:T(8,128)}, f32[394,768]{1,0:T(8,128)S(1)}, u32[]{:S(2)}) copy-start(f32[394,768]{1,0:T(8,128)S(1)} %get-tuple-element.90) | copy-start | bytes 3631108
  112.5 2.3 copy-start.35
  112.5 2.3 copy-start.37
  114.8 2.4 copy-start.25
  114.8 2.4 copy-start.34
  117.1 2.9 %copy-start.29 = (bf16[394,768]{1,0:T(8,128)(2,1)S(1)}, bf16[394,768]{1,0:T(8,128)(2,1)}, u32[]{:S(2)}) copy-start(bf16[394,768]{1,0:T(8,128)(2,1)} %param.17) | copy-start | bytes 1815556
  117.2 2.9 %copy-start.43 = (bf16[16,48,1536]{2,1,0:T(8,128)(2,1)S(1)}, bf16[16,48,1536]{2,1,0:T(8,128)(2,1)}, u32[]{:S(2)}) copy-start(bf16[16,48,1536]{2,1,0:T(8,128)(2,1)} %get-tuple-element.29) | copy-start | bytes 7077892
  121.8 1.2 copy-start.49
  121.9 2.1 copy-start.41
  125.9 1.6 copy-start.53
  128.1 1.3 copy-start.3
  128.2 2.5 copy-start.27
  129.4 13.0 %slice-start = ((s8[4915200]{0:T(1024)(128)(4,1)}), s8[720896]{0:T(1024)(128)(4,1)S(1)}, s32[]{:S(2)}) async-start(s8[4915200]{0:T(1024)(128)(4,1)} %bitcast.125), calls=%async_computation | async-start | bytes 1441792
  138.3 4.1 %slice-start.1 = ((s8[4915200]{0:T(1024)(128)(4,1)}), s8[4194304]{0:T(1024)(128)(4,1)S(1)}, s32[]{:S(2)}) async-start(s8[4915200]{0:T(1024)(128)(4,1)} %bitcast.125), calls=%async_computation.1 | async-start | bytes 8388608
  138.6 3.8 %copy-start.7 = (bf16[2,197,1,6,64]{1,4,3,0,2:T(8,128)(2,1)S(1)}, bf16[2,197,1,6,64]{1,4,3,0,2:T(8,128)(2,1)}, u32[]{:S(2)}) copy-start(bf16[2,197,1,6,64]{1,4,3,0,2:T(8,128)(2,1)} %copy-done.6) | copy-start | bytes 907780
  142.4 1.6 copy-start.17
  142.4 1.6 copy-start.19
  144.1 1.0 copy-start.9
  144.1 1.1 copy-start.11
  145.2 1.1 copy-start.26
  145.2 1.5 copy-start.54
  146.7 2.9 %copy-start.21 = (bf16[394,384]{0,1:T(8,128)(2,1)S(1)}, bf16[394,384]{0,1:T(8,128)(2,1)}, u32[]{:S(2)}) copy-start(bf16[394,384]{0,1:T(8,128)(2,1)} %copy-done.20) | copy-start | bytes 907780
  146.7 2.9 %copy-start.28 = (bf16[394,768]{1,0:T(8,128)(2,1)S(1)}, bf16[394,768]{1,0:T(8,128)(2,1)}, u32[]{:S(2)}) copy-start(bf16[394,768]{1,0:T(8,128)(2,1)} %copy-done.27) | copy-start | bytes 1815556
  149.6 1.5 copy-start.50
  151.0 1.4 copy-start.22
  162.1 4.2 %copy-start.24 = (bf16[394,1152]{0,1:T(8,128)(2,1)S(1)}, bf16[394,1152]{0,1:T(8,128)(2,1)}, u32[]{:S(2)}) copy-start(bf16[394,1152]{0,1:T(8,128)(2,1)} %reshape.198) | copy-start | bytes 2723332
  176.8 2.9 %copy-start.23 = (bf16[394,1152]{0,1:T(8,128)(2,1)S(1)}, bf16[394,1152]{0,1:T(8,128)(2,1)}, u32[]{:S(2)}) copy-start(bf16[394,1152]{0,1:T(8,128)(2,1)} %reshape.199) | copy-start | bytes 2723332
  176.8 2.9 %copy-start.45 = (bf16[16,48,1152]{2,1,0:T(8,128)(2,1)S(1)}, bf16[16,48,1152]{2,1,0:T(8,128)(2,1)}, u32[]{:S(2)}) copy-start(bf16[16,48,1152]{2,1,0:T(8,128)(2,1)} %get-tuple-element.26) | copy-start | bytes 5308420
  176.8 2.9 %copy-start.52 = (f32[394,768]{1,0:T(8,128)S(1)}, f32[394,768]{1,0:T(8,128)}, u32[]{:S(2)}) copy-start(f32[394,768]{1,0:T(8,128)} %fusion.87) | copy-start | bytes 3631108
  179.8 1.8 copy-start.30
  179.8 1.8 copy-start.51
  181.6 3.0 %copy-start.48 = (bf16[394,1536]{1,0:T(8,128)(2,1)S(1)}, bf16[394,1536]{1,0:T(8,128)(2,1)}, u32[]{:S(2)}) copy-start(bf16[394,1536]{1,0:T(8,128)(2,1)} %get-tuple-element.91) | copy-start | bytes 3631108
  184.6 3.0 %copy-start.31 = (bf16[768,384]{1,0:T(8,128)(2,1)S(1)}, bf16[768,384]{1,0:T(8,128)(2,1)}, u32[]{:S(2)}) copy-start(bf16[768,384]{1,0:T(8,128)(2,1)} %convolution_convert_fusion.7) | copy-start | bytes 1769476
  187.5 2.3 copy-start.15
  187.5 2.4 copy-start.32
  190.2 85.3 %copy-start.44 = (bf16[16,48,1536]{2,1,0:T(8,128)(2,1)S(1)}, bf16[16,48,1536]{2,1,0:T(8,128)(2,1)}, u32[]{:S(2)}) copy-start(bf16[16,48,1536]{2,1,0:T(8,128)(2,1)} %get-tuple-element.29) | copy-start | bytes 7077892
  275.4 1.8 copy-start.2
  275.4 2.0 copy-start.42
  275.4 2.0 copy-start.47
  277.5 2.7 copy-start.4
